TPU v7x, 32 devices: a whole 2x2x4 slice. The times are simulated.
32 devices in a mesh: member: 2 (over y), lat: 4 (over z), lon: 2 (over x), lev: 2 (over core).
Axes of the slice: x: 2, y: 2, z: 4, core: 2. Of those that a mesh axis runs over, the one named last changes fastest.
Arguments:
- adjoint_in: float32 [10, 16, 32, 1152], P('member', 'lev', 'lat', 'lon'), parts along dimension 0, may hold values from -12 to 12
- lat_ahead: float32 [32, 32, 1152], P(('member', 'lev'), 'lat', 'lon'), parts along dimension 0, may hold values from 0.35 to 0.8
- lat_behind: float32 [32, 32, 1152], P(('member', 'lev'), 'lat', 'lon'), parts along dimension 0, may hold values from 0.02 to 0.06
- lon_ahead: float32 [32, 32, 1152], P(('member', 'lev'), 'lat', 'lon'), parts along dimension 0, may hold values from 0.02 to 0.06
- lon_behind: float32 [32, 32, 1152], P(('member', 'lev'), 'lat', 'lon'), parts along dimension 0, may hold values from 0.02 to 0.06
- coupling: float32 [16, 5, 5], P('lev'), may hold values from -0.9 to 0.9
- cutoff: int32 [32], replicated, may hold values from 1 to 576, as said below
Outputs:
- adjoint_out: float32 [10, 16, 32, 1152], P('member', 'lev', 'lat', 'lon'), parts along dimension 0
There are 2 independent parts, one for each index of `member`. A program takes and returns all parts, laid end to end along the dimension named above; an argument that names none is the same for every part. Nothing has to cross between parts.
Inputs may be any that keep to these rules, and one draw needn't show every extreme that they name: Rows 8 to 23 have a cutoff of exactly 576, every other row a cutoff below 576; the first and the last row have cutoff 1.
All inputs are finite; a program needn't handle non-finite values.
Results may differ from a plain program's by a relative error of at most 0.00011.
Values sent between devices are 32-bit elements; how exact they have to be, the bound alone decides.
A program may use at most 64 MiB of HBM per device.

v0:
```python
import functools

import jax
import jax.numpy as jnp
import numpy as np
from jax import lax
from jax.experimental import pallas as pl
from jax.experimental.pallas import tpu as pltpu
from jax.sharding import PartitionSpec as P

SUBSTEPS = 6
DEPTH = 1
RIM = 16
LANES = 128
MESH = pl.DeviceIdType.MESH


def split_parts(table):
    high = table.astype(jnp.bfloat16)
    low = (table - high.astype(np.float32)).astype(jnp.bfloat16)
    return np.stack([high, low])


def tables(circle, sector, width):
    column = np.arange(circle)
    middle = circle // 2
    wavenumber = np.where(column <= middle, column, column - middle)
    position = np.arange(circle)
    phase = (position[:, None] * wavenumber[None, :]) % circle
    angle = phase * (2.0 * np.pi / circle)
    weight = np.where((column == 0) | (column == middle), 1.0 / circle, 2.0 / circle)
    basis = np.where((column <= middle)[None, :], np.cos(angle), np.sin(angle))
    basis = (basis * np.sqrt(weight)[None, :]).astype(np.float32)
    lane = np.arange(width)
    target = np.where(lane < sector + RIM, lane, lane - width) % circle
    return split_parts(basis), split_parts(np.ascontiguousarray(basis[target].T)), wavenumber


def halves(values):
    high = values.astype(jnp.bfloat16)
    low = (values - high.astype(jnp.float32)).astype(jnp.bfloat16)
    return high, low


def product(values, high_table, low_table):
    high, low = halves(values)
    dot = functools.partial(jnp.dot, preferred_element_type=jnp.float32)
    return dot(high, high_table) + (dot(high, low_table) + dot(low, high_table))


def kernel(
    peers, bands, fields, rows, levels, sector, width,
    x_ref, rate_refs, couple_ref, damp_ref, forward_hbm, inverse_hbm, out_ref,
    forward, inverse, swapped, spectra, filtered, rate_rows, packed, rim, rates, coefs, power, state,
    table_sem, swap_send, swap_recv, rim_send, rim_recv, rate_send, rate_recv, edge_send, edge_recv,
):
    chunks = 2
    lat = lax.axis_index("lat")
    lon = lax.axis_index("lon")
    quarter = bands // 4
    polar = (lat < quarter) | (lat >= 3 * quarter)
    has_prev = lat > 0
    has_next = lat < bands - 1
    plane = rows * levels
    part = plane // chunks
    tail = sector % LANES
    body = sector - tail

    def lon_id(d):
        return {"lon": lax.rem(lon + d + peers, peers)}

    barrier = pltpu.get_barrier_semaphore()
    for d in range(1, peers):
        pl.semaphore_signal(barrier, inc=1, device_id=lon_id(d), device_id_type=MESH)

    @pl.when(has_prev)
    def _():
        pl.semaphore_signal(barrier, inc=1, device_id={"lat": lat - 1}, device_id_type=MESH)

    @pl.when(has_next)
    def _():
        pl.semaphore_signal(barrier, inc=1, device_id={"lat": lat + 1}, device_id_type=MESH)

    table_copies = [
        pltpu.make_async_copy(forward_hbm, forward, table_sem.at[0]),
        pltpu.make_async_copy(inverse_hbm, inverse, table_sem.at[1]),
    ]

    @pl.when(polar)
    def _():
        for copy in table_copies:
            copy.start()

    sources = [r for r in rate_refs] + [x_ref.at[f] for f in range(fields)]
    lane = lax.broadcasted_iota(jnp.int32, (plane, LANES), 1)
    for block in range(packed.shape[0]):
        value = jnp.zeros((plane, LANES), jnp.float32)
        for k, source in enumerate(sources[4 * block:4 * block + 4]):
            first = source[:, 0:LANES]
            last = jnp.concatenate(
                [source[:, body:sector], jnp.zeros((plane, LANES - tail), jnp.float32)], axis=1
            )
            base = 32 * k
            if base:
                first = pltpu.roll(first, base, 1)
            last = pltpu.roll(last, (base + RIM - (tail - RIM)) % LANES, 1)
            value = jnp.where((lane >= base) & (lane < base + RIM), first, value)
            value = jnp.where((lane >= base + RIM) & (lane < base + 2 * RIM), last, value)
        packed[block] = value

    greeters = peers - 1 + has_prev.astype(jnp.int32) + has_next.astype(jnp.int32)
    pl.semaphore_wait(barrier, greeters)

    rim_slots = rim.shape[0]
    rim_copies = [
        pltpu.make_async_remote_copy(
            src_ref=packed, dst_ref=rim.at[slot], send_sem=rim_send.at[slot],
            recv_sem=rim_recv.at[slot], device_id=lon_id(-1 if slot == 0 else 1), device_id_type=MESH,
        )
        for slot in range(rim_slots)
    ]
    for copy in rim_copies:
        copy.start()

    swaps = [
        [
            pltpu.make_async_remote_copy(
                src_ref=x_ref.at[:, pl.ds(c * part, part)],
                dst_ref=swapped.at[d - 1, :, pl.ds(c * part, part)],
                send_sem=swap_send.at[c, d - 1], recv_sem=swap_recv.at[c, d - 1],
                device_id=lon_id(-d), device_id_type=MESH,
            )
            for d in range(1, peers)
        ]
        for c in range(chunks)
    ]

    @pl.when(polar)
    def _():
        for c in range(chunks):
            for copy in swaps[c]:
                copy.start()

    def entry(g, f):
        value = couple_ref[g * fields + f]
        return value + 1.0 if g == f else value

    once = [[entry(g, f) for f in range(fields)] for g in range(fields)]

    def multiply(a, b):
        return [
            [sum(a[g][h] * b[h][f] for h in range(fields)) for f in range(fields)]
            for g in range(fields)
        ]

    result = once
    for _ in range(SUBSTEPS - 1):
        result = multiply(result, once)
    for g in range(fields):
        for f in range(fields):
            power[g * fields + f] = result[g][f]

    depth = DEPTH

    @pl.when(jnp.logical_not(has_prev))
    def _():
        rates[:, 0:depth] = jnp.zeros((4, depth, levels, width), jnp.float32)
        for s in range(0, SUBSTEPS, depth):
            state[s, :, 0:depth] = jnp.zeros((fields, depth, levels, width), jnp.float32)

    @pl.when(jnp.logical_not(has_next))
    def _():
        rates[:, depth + rows:] = jnp.zeros((4, depth, levels, width), jnp.float32)
        for s in range(0, SUBSTEPS, depth):
            state[s, :, depth + rows:] = jnp.zeros((fields, depth, levels, width), jnp.float32)

    for copy in rim_copies:
        copy.wait()

    def with_rim(index, target):
        source = sources[index]
        block, base = index // 4, 32 * (index % 4)
        east = pltpu.roll(rim[0, block], (tail - base) % LANES, 1)
        west = pltpu.roll(rim[rim_slots - 1, block], (LANES - RIM - base - RIM) % LANES, 1)
        last = jnp.concatenate(
            [source[:, body:sector], jnp.zeros((plane, LANES - tail), jnp.float32)], axis=1
        )
        last = jnp.where((lane >= tail) & (lane < tail + RIM), east, last)
        last = jnp.where(lane >= LANES - RIM, west, last)
        for t in range(body // LANES):
            target[t] = source[:, t * LANES:(t + 1) * LANES]
        target[body // LANES] = last

    def row_of(ref, j):
        return jnp.concatenate(
            [ref[t, pl.ds(j, levels, rows), :] for t in range(width // LANES)], axis=1
        )

    for r in range(4):
        with_rim(r, rate_rows.at[r])
    for r in range(4):
        for j in range(rows):
            rates[r, depth + j] = row_of(rate_rows.at[r], j)

    def to_neighbours(ref, send, recv):
        to_prev = pltpu.make_async_remote_copy(
            src_ref=ref.at[:, pl.ds(depth, depth)], dst_ref=ref.at[:, pl.ds(depth + rows, depth)],
            send_sem=send.at[0], recv_sem=recv.at[0],
            device_id={"lat": lat - 1}, device_id_type=MESH,
        )
        to_next = pltpu.make_async_remote_copy(
            src_ref=ref.at[:, pl.ds(rows, depth)], dst_ref=ref.at[:, pl.ds(0, depth)],
            send_sem=send.at[1], recv_sem=recv.at[1],
            device_id={"lat": lat + 1}, device_id_type=MESH,
        )

        def start():
            pl.when(has_prev)(to_prev.start)
            pl.when(has_next)(to_next.start)

        def arrive():
            pl.when(has_next)(to_prev.wait_recv)
            pl.when(has_prev)(to_next.wait_recv)

        def sent():
            pl.when(has_prev)(to_prev.wait_send)
            pl.when(has_next)(to_next.wait_send)

        return start, arrive, sent

    rate_start, rate_arrive, rate_sent = to_neighbours(rates, rate_send, rate_recv)
    rate_start()

    @pl.when(jnp.logical_not(polar))
    def _():
        for f in range(fields):
            with_rim(4 + f, filtered.at[f])

    modes = peers * sector

    @pl.when(polar)
    def _():
        for copy in table_copies:
            copy.wait()
        for c in range(chunks):
            own = x_ref[:, c * part:(c + 1) * part].reshape(fields * part, sector)
            spectra[c] = product(own, forward[0, 0:sector], forward[1, 0:sector])
        for c in range(chunks):
            for copy in swaps[c]:
                copy.wait_recv()
            total = spectra[c]
            for d in range(1, peers):
                values = swapped[d - 1, :, c * part:(c + 1) * part].reshape(fields * part, sector)
                start, end = d * sector, (d + 1) * sector
                total = total + product(values, forward[0, start:end], forward[1, start:end])
            damped = total.reshape(fields * part // rows, rows, modes) * damp_ref[...][None]
            result = product(damped.reshape(fields * part, modes), inverse[0], inverse[1])
            for t in range(width // LANES):
                block = result[:, t * LANES:(t + 1) * LANES].reshape(fields, part, LANES)
                filtered[:, t, c * part:(c + 1) * part] = block

    edges = [
        to_neighbours(state.at[s], edge_send.at[s // depth], edge_recv.at[s // depth])
        for s in range(0, SUBSTEPS, depth)
    ]

    def couple(j):
        values = [row_of(filtered.at[g], j) for g in range(fields)]
        for f in range(fields):
            total = None
            for g in range(fields):
                term = jnp.tile(power[g * fields + f], (1, width // LANES)) * values[g]
                total = term if total is None else total + term
            state[0, f, depth + j] = total

    outer = list(range(depth)) + list(range(rows - depth, rows))
    inner = list(range(depth, rows - depth))
    for j in outer:
        couple(j)
    edges[0][0]()
    for j in inner:
        couple(j)

    rate_arrive()
    below_last = jnp.where(has_next, 1.0, 0.0)
    for j in range(1, rows + 2 * depth - 1):
        north = rates[0, j]
        if j == depth + rows - 1:
            north = north * below_last
        south = rates[1, j - 1]
        east = rates[2, j]
        west = pltpu.roll(rates[3, j], 1, 1)
        coefs[0, j] = 1.0 - east - west - north - south
        coefs[1, j] = east
        coefs[2, j] = west
        coefs[3, j] = north
        coefs[4, j] = south

    def advance(s, j):
        rate = [coefs[k, j] for k in range(5)]
        for f in range(fields):
            here = state[s, f, j]
            value = (
                rate[0] * here
                + rate[1] * pltpu.roll(here, width - 1, 1)
                + rate[2] * pltpu.roll(here, 1, 1)
                + rate[3] * state[s, f, j + 1]
                + rate[4] * state[s, f, j - 1]
            )
            state[s + 1, f, j] = value

    def advance_rows(s, start, end):
        if end > start:
            @pl.loop(start, end)
            def _(j):
                advance(s, j)

    for s in range(SUBSTEPS):
        reach = depth - 1 - s % depth
        begin, end = depth - reach, depth + rows + reach
        if s % depth == 0:
            edges[s // depth][1]()
        if (s + 1) % depth == 0 and s + 1 < SUBSTEPS:
            advance_rows(s, depth, 2 * depth)
            advance_rows(s, rows, rows + depth)
            edges[(s + 1) // depth][0]()
            advance_rows(s, 2 * depth, rows)
        else:
            advance_rows(s, begin, end)

    for f in range(fields):
        for j in range(rows):
            value = state[SUBSTEPS, f, depth + j]
            for t in range(width // LANES):
                filtered[f, t, pl.ds(j, levels, rows), :] = value[:, t * LANES:(t + 1) * LANES]
    for t in range(width // LANES):
        end = min(sector, (t + 1) * LANES)
        out_ref[:, :, t * LANES:end] = filtered[:, t, :, 0:end - t * LANES]

    rate_sent()
    for edge in edges:
        edge[2]()

    @pl.when(polar)
    def _():
        for c in range(chunks):
            for copy in swaps[c]:
                copy.wait_send()


def shards(peers, bands, adjoint_in, lat_ahead, lat_behind, lon_ahead, lon_behind, coupling, cutoff):
    fields, levels, rows, sector = adjoint_in.shape
    width = -(-(sector + 2 * RIM) // LANES) * LANES
    circle = sector * peers
    forward, inverse, wavenumber = tables(circle, sector, width)
    plane = rows * levels
    limits = lax.dynamic_slice_in_dim(cutoff, lax.axis_index("lat") * rows, rows, 0)
    limit = limits.astype(jnp.float32)[:, None]
    number = jnp.asarray(wavenumber, jnp.float32)[None, :]
    ratio = limit / jnp.maximum(number, 1.0)
    damping = jnp.where(number > limit, ratio * ratio, 1.0)
    couple = jnp.broadcast_to(
        jnp.transpose(coupling, (1, 2, 0)).reshape(fields * fields, levels, 1), (fields * fields, levels, LANES)
    )
    flat = [r.reshape(plane, sector) for r in (lat_ahead, lat_behind, lon_ahead, lon_behind)]
    vmem = pl.BlockSpec(memory_space=pltpu.VMEM)
    anywhere = pl.BlockSpec(memory_space=pl.ANY)
    rim_slots = 1 if peers == 2 else 2
    packs = -(-(4 + fields) // 4)
    tall = rows + 2 * DEPTH
    rounds = SUBSTEPS // DEPTH

    def body(x, a, b, c, d, *rest):
        kernel(peers, bands, fields, rows, levels, sector, width, x, [a, b, c, d], *rest)

    dma = pltpu.SemaphoreType.DMA
    out = pl.pallas_call(
        body,
        out_shape=jax.ShapeDtypeStruct((fields, plane, sector), jnp.float32),
        in_specs=[vmem] * 7 + [anywhere] * 2,
        out_specs=vmem,
        scratch_shapes=[
            pltpu.VMEM(forward.shape, jnp.bfloat16),
            pltpu.VMEM(inverse.shape, jnp.bfloat16),
            pltpu.VMEM((peers - 1, fields, plane, sector), jnp.float32),
            pltpu.VMEM((2, fields * plane // 2, circle), jnp.float32),
            pltpu.VMEM((fields, width // LANES, plane, LANES), jnp.float32),
            pltpu.VMEM((4, width // LANES, plane, LANES), jnp.float32),
            pltpu.VMEM((packs, plane, LANES), jnp.float32),
            pltpu.VMEM((rim_slots, packs, plane, LANES), jnp.float32),
            pltpu.VMEM((4, tall, levels, width), jnp.float32),
            pltpu.VMEM((5, tall, levels, width), jnp.float32),
            pltpu.VMEM((fields * fields, levels, LANES), jnp.float32),
            pltpu.VMEM((SUBSTEPS + 1, fields, tall, levels, width), jnp.float32),
            dma((2,)), dma((2, peers - 1)), dma((2, peers - 1)),
            dma((rim_slots,)), dma((rim_slots,)),
            dma((2,)), dma((2,)), dma((rounds, 2)), dma((rounds, 2)),
        ],
        compiler_params=pltpu.CompilerParams(
            collective_id=0, has_side_effects=True, vmem_limit_bytes=48 * 1024 * 1024
        ),
    )(adjoint_in.reshape(fields, plane, sector), *flat, couple, damping, jnp.asarray(forward), jnp.asarray(inverse))
    return out.reshape(fields, levels, rows, sector)


def solution(mesh):
    placed = (
        P("member", "lev", "lat", "lon"),
        P(("member", "lev"), "lat", "lon"),
        P(("member", "lev"), "lat", "lon"),
        P(("member", "lev"), "lat", "lon"),
        P(("member", "lev"), "lat", "lon"),
        P("lev", None, None),
        P(),
    )
    return jax.shard_map(
        functools.partial(shards, mesh.shape["lon"], mesh.shape["lat"]),
        mesh=mesh,
        in_specs=placed,
        out_specs=P("member", "lev", "lat", "lon"),
        check_vma=False,
    )
```

profile of v0, /device:TPU:0, one launch (start us, length us, event | category | flops | bytes accessed | tf_op | source)
XLA Modules:
  0.0 63.7 jit_solution(17090419682941510350)
XLA Ops:
  0.0 0.7 %dynamic-slice_convert_fusion = f32[8]{0:T(128)S(1)} fusion(s32[32]{0:T(128)} %param.16, s32[]{:T(128)S(6)} %select_n.7), kind=kLoop, calls=%fused_computation.2 | loop fusion | flops 8 | bytes 68 | tf_op jit(solution)/shard_map/convert_element_type | solution.py:358
  0.7 0.8 %copy.11 = f32[5,5,8]{2,1,0:T(8,128)S(1)} copy(f32[5,5,8]{1,2,0:T(8,128)} %bitcast.13) | data formatting | bytes 1600 | tf_op jit(solution)/shard_map/transpose | solution.py:363
  1.6 0.8 %fusion.rest_1_ = f32[8,1152]{1,0:T(8,128)S(1)} fusion(f32[1152]{0:T(1024)} %constant.25, f32[1152]{0:T(1024)} %constant.20.clone, f32[8]{0:T(128)S(1)} %dynamic-slice_convert_fusion), kind=kLoop, calls=%fused_computation.1 | loop fusion | flops 36864 | bytes 46112 | tf_op jit(solution)/shard_map/jit(_where)/select_n | solution.py:361
  2.4 0.1 broadcast_in_dim.14.rest_0_
  2.4 0.0 copy-start
  2.5 1.8 %copy-done = bf16[2,1152,640]{2,1,0:T(8,128)(2,1)S(1)} copy-done((bf16[2,1152,640]{2,1,0:T(8,128)(2,1)S(1)}, bf16[2,1152,640]{2,1,0:T(8,128)(2,1)}, u32[]{:S(2)}) %copy-start) | copy-done | bytes 2949144
  4.3 0.0 copy-start.1
  4.3 1.1 %copy-done.1 = f32[5,8,8,576]{3,2,1,0:T(8,128)S(1)} copy-done((f32[5,8,8,576]{3,2,1,0:T(8,128)S(1)}, f32[5,8,8,576]{3,2,1,0:T(8,128)}, u32[]{:S(2)}) %copy-start.1) | copy-done | bytes 737304
  5.4 0.0 copy-start.2
  5.4 0.9 %copy-done.2 = f32[8,8,576]{2,1,0:T(8,128)S(1)} copy-done((f32[8,8,576]{2,1,0:T(8,128)S(1)}, f32[8,8,576]{2,1,0:T(8,128)}, u32[]{:S(2)}) %copy-start.2) | copy-done | bytes 147480
  6.3 0.0 copy-start.3
  6.3 0.9 %copy-done.3 = f32[8,8,576]{2,1,0:T(8,128)S(1)} copy-done((f32[8,8,576]{2,1,0:T(8,128)S(1)}, f32[8,8,576]{2,1,0:T(8,128)}, u32[]{:S(2)}) %copy-start.3) | copy-done | bytes 147480
  7.3 0.0 copy-start.4
  7.3 0.9 %copy-done.4 = f32[8,8,576]{2,1,0:T(8,128)S(1)} copy-done((f32[8,8,576]{2,1,0:T(8,128)S(1)}, f32[8,8,576]{2,1,0:T(8,128)}, u32[]{:S(2)}) %copy-start.4) | copy-done | bytes 147480
  8.2 0.0 copy-start.5
  8.2 0.9 %copy-done.5 = f32[8,8,576]{2,1,0:T(8,128)S(1)} copy-done((f32[8,8,576]{2,1,0:T(8,128)S(1)}, f32[8,8,576]{2,1,0:T(8,128)}, u32[]{:S(2)}) %copy-start.5) | copy-done | bytes 147480
  9.1 53.8 %shard_map.100 = f32[5,64,576]{2,1,0:T(8,128)S(1)} custom-call(f32[5,64,576]{2,1,0:T(8,128)S(1)} %bitcast.8, f32[64,576]{1,0:T(8,128)S(1)} %bitcast.9, f32[64,576]{1,0:T(8,128)S(1)} %bitcast.10, f32[64,576]{1,0:T(8,128)S(1)} %bitcast.11, f32[64,576]{1,0:T(8,128)S(1)} %bitcast.12, f32[25,8,128]{2,1,0:T(8,128)S(1)} %broadcast_in_dim.14.rest_0_, ...), custom_call_target="tpu_custom_call" | custom-call | tf_op jit(solution)/shard_map/pallas_call | solution.py:377
  62.9 0.9 %copy.13 = f32[5,8,8,576]{3,2,1,0:T(8,128)} copy(f32[5,8,8,576]{3,2,1,0:T(8,128)S(1)} %bitcast.7) | data formatting | bytes 1474560
  (1 shorter events, 0.0 us)
Async XLA Ops:
  2.4 1.8 %copy-start = (bf16[2,1152,640]{2,1,0:T(8,128)(2,1)S(1)}, bf16[2,1152,640]{2,1,0:T(8,128)(2,1)}, u32[]{:S(2)}) copy-start(bf16[2,1152,640]{2,1,0:T(8,128)(2,1)} %constant.22.clone.rest_3_) | copy-start | bytes 8847364
  4.3 1.1 %copy-start.1 = (f32[5,8,8,576]{3,2,1,0:T(8,128)S(1)}, f32[5,8,8,576]{3,2,1,0:T(8,128)}, u32[]{:S(2)}) copy-start(f32[5,8,8,576]{3,2,1,0:T(8,128)} %param.10) | copy-start | bytes 2211844
  5.4 0.9 %copy-start.2 = (f32[8,8,576]{2,1,0:T(8,128)S(1)}, f32[8,8,576]{2,1,0:T(8,128)}, u32[]{:S(2)}) copy-start(f32[8,8,576]{2,1,0:T(8,128)} %param.11) | copy-start | bytes 442372
  6.3 0.9 %copy-start.3 = (f32[8,8,576]{2,1,0:T(8,128)S(1)}, f32[8,8,576]{2,1,0:T(8,128)}, u32[]{:S(2)}) copy-start(f32[8,8,576]{2,1,0:T(8,128)} %param.12) | copy-start | bytes 442372
  7.3 0.9 %copy-start.4 = (f32[8,8,576]{2,1,0:T(8,128)S(1)}, f32[8,8,576]{2,1,0:T(8,128)}, u32[]{:S(2)}) copy-start(f32[8,8,576]{2,1,0:T(8,128)} %param.13) | copy-start | bytes 442372
  8.2 0.9 %copy-start.5 = (f32[8,8,576]{2,1,0:T(8,128)S(1)}, f32[8,8,576]{2,1,0:T(8,128)}, u32[]{:S(2)}) copy-start(f32[8,8,576]{2,1,0:T(8,128)} %param.14) | copy-start | bytes 442372
where the time goes:
time: 64.1 us; the launch traced here: 63.7 us
  Pallas kernels  53.8 us (84%)
  local copies, waits for them, and re-layouts  8.44 us (13%)
  other arithmetic  1.52 us (2%)
    pallas_call x1, Pallas kernels, shards(): pl.pallas_call(body, out_shape=jax.ShapeDtypeStruct((fields, plane, secto...  53.8 us
    unnamed x13, local copies, waits for them, and re-layouts  7.53 us

commit v1 on v0

--- a/solution.py
+++ b/solution.py
@@ -9,7 +9,7 @@
 from jax.sharding import PartitionSpec as P
 
 SUBSTEPS = 6
-DEPTH = 1
+DEPTH = 3
 RIM = 16
 LANES = 128
 MESH = pl.DeviceIdType.MESH
@@ -33,7 +33,7 @@
     basis = (basis * np.sqrt(weight)[None, :]).astype(np.float32)
     lane = np.arange(width)
     target = np.where(lane < sector + RIM, lane, lane - width) % circle
-    return split_parts(basis), split_parts(np.ascontiguousarray(basis[target].T)), wavenumber
+    return split_parts(basis), split_parts(np.ascontiguousarray(basis[target].T))
 
 
 def halves(values):
@@ -50,9 +50,9 @@
 
 def kernel(
     peers, bands, fields, rows, levels, sector, width,
-    x_ref, rate_refs, couple_ref, damp_ref, forward_hbm, inverse_hbm, out_ref,
-    forward, inverse, swapped, spectra, filtered, rate_rows, packed, rim, rates, coefs, power, state,
-    table_sem, swap_send, swap_recv, rim_send, rim_recv, rate_send, rate_recv, edge_send, edge_recv,
+    x_hbm, rates_hbm, couple_ref, cutoff_ref, forward_hbm, inverse_hbm, out_ref,
+    x_ref, rate_ref, forward, inverse, swapped, spectra, filtered, rate_rows, packed, rim, rates, coefs, power, state, damp_ref,
+    load_sem, table_sem, swap_send, swap_recv, rim_send, rim_recv, rate_send, rate_recv, edge_send, edge_recv,
 ):
     chunks = 2
     lat = lax.axis_index("lat")
@@ -81,6 +81,12 @@
     def _():
         pl.semaphore_signal(barrier, inc=1, device_id={"lat": lat + 1}, device_id_type=MESH)
 
+    rate_refs = [rate_ref.at[r] for r in range(4)]
+    loads = [pltpu.make_async_copy(x_hbm, x_ref, load_sem.at[4])]
+    loads += [pltpu.make_async_copy(rates_hbm[r], rate_ref.at[r], load_sem.at[r]) for r in range(4)]
+    for copy in loads:
+        copy.start()
+
     table_copies = [
         pltpu.make_async_copy(forward_hbm, forward, table_sem.at[0]),
         pltpu.make_async_copy(inverse_hbm, inverse, table_sem.at[1]),
@@ -90,6 +96,30 @@
     def _():
         for copy in table_copies:
             copy.start()
+
+    greeters = peers - 1 + has_prev.astype(jnp.int32) + has_next.astype(jnp.int32)
+    pl.semaphore_wait(barrier, greeters)
+
+    swaps = [
+        [
+            pltpu.make_async_remote_copy(
+                src_ref=x_hbm.at[:, pl.ds(c * part, part)],
+                dst_ref=swapped.at[d - 1, :, pl.ds(c * part, part)],
+                send_sem=swap_send.at[c, d - 1], recv_sem=swap_recv.at[c, d - 1],
+                device_id=lon_id(-d), device_id_type=MESH,
+            )
+            for d in range(1, peers)
+        ]
+        for c in range(chunks)
+    ]
+
+    @pl.when(polar)
+    def _():
+        for copy in swaps[0]:
+            copy.start()
+
+    for copy in loads:
+        copy.wait()
 
     sources = [r for r in rate_refs] + [x_ref.at[f] for f in range(fields)]
     lane = lax.broadcasted_iota(jnp.int32, (plane, LANES), 1)
@@ -108,42 +138,40 @@
             value = jnp.where((lane >= base + RIM) & (lane < base + 2 * RIM), last, value)
         packed[block] = value
 
-    greeters = peers - 1 + has_prev.astype(jnp.int32) + has_next.astype(jnp.int32)
-    pl.semaphore_wait(barrier, greeters)
-
     rim_slots = rim.shape[0]
-    rim_copies = [
-        pltpu.make_async_remote_copy(
-            src_ref=packed, dst_ref=rim.at[slot], send_sem=rim_send.at[slot],
-            recv_sem=rim_recv.at[slot], device_id=lon_id(-1 if slot == 0 else 1), device_id_type=MESH,
-        )
-        for slot in range(rim_slots)
-    ]
-    for copy in rim_copies:
+
+    def rim_copies(stage, start, stop):
+        return [
+            pltpu.make_async_remote_copy(
+                src_ref=packed.at[start:stop], dst_ref=rim.at[slot, start:stop],
+                send_sem=rim_send.at[stage, slot], recv_sem=rim_recv.at[stage, slot],
+                device_id=lon_id(-1 if slot == 0 else 1), device_id_type=MESH,
+            )
+            for slot in range(rim_slots)
+        ]
+
+    rate_rims, field_rims = rim_copies(0, 0, 1), rim_copies(1, 1, packed.shape[0])
+    for copy in rate_rims:
         copy.start()
 
-    swaps = [
-        [
-            pltpu.make_async_remote_copy(
-                src_ref=x_ref.at[:, pl.ds(c * part, part)],
-                dst_ref=swapped.at[d - 1, :, pl.ds(c * part, part)],
-                send_sem=swap_send.at[c, d - 1], recv_sem=swap_recv.at[c, d - 1],
-                device_id=lon_id(-d), device_id_type=MESH,
-            )
-            for d in range(1, peers)
-        ]
-        for c in range(chunks)
-    ]
-
     @pl.when(polar)
     def _():
-        for c in range(chunks):
+        for c in range(1, chunks):
             for copy in swaps[c]:
                 copy.start()
 
+    @pl.when(jnp.logical_not(polar))
+    def _():
+        for copy in field_rims:
+            copy.start()
+
+    level_of = lax.broadcasted_iota(jnp.int32, (levels, LANES), 0)
+
     def entry(g, f):
-        value = couple_ref[g * fields + f]
-        return value + 1.0 if g == f else value
+        value = jnp.full((levels, LANES), 1.0 if g == f else 0.0, jnp.float32)
+        for level in range(levels):
+            value = jnp.where(level_of == level, value + couple_ref[level * fields * fields + g * fields + f], value)
+        return value
 
     once = [[entry(g, f) for f in range(fields)] for g in range(fields)]
 
@@ -174,7 +202,7 @@
         for s in range(0, SUBSTEPS, depth):
             state[s, :, depth + rows:] = jnp.zeros((fields, depth, levels, width), jnp.float32)
 
-    for copy in rim_copies:
+    for copy in rate_rims:
         copy.wait()
 
     def with_rim(index, target):
@@ -233,6 +261,8 @@
 
     @pl.when(jnp.logical_not(polar))
     def _():
+        for copy in field_rims:
+            copy.wait()
         for f in range(fields):
             with_rim(4 + f, filtered.at[f])
 
@@ -240,6 +270,14 @@
 
     @pl.when(polar)
     def _():
+        column = lax.broadcasted_iota(jnp.int32, (rows, modes), 1)
+        row_index = lax.broadcasted_iota(jnp.int32, (rows, modes), 0)
+        number = jnp.where(column <= modes // 2, column, column - modes // 2).astype(jnp.float32)
+        limit = jnp.zeros((rows, modes), jnp.float32)
+        for j in range(rows):
+            limit = jnp.where(row_index == j, cutoff_ref[lat * rows + j].astype(jnp.float32), limit)
+        ratio = limit / jnp.maximum(number, 1.0)
+        damp_ref[...] = jnp.where(number > limit, ratio * ratio, 1.0)
         for copy in table_copies:
             copy.wait()
         for c in range(chunks):
@@ -352,19 +390,12 @@
     fields, levels, rows, sector = adjoint_in.shape
     width = -(-(sector + 2 * RIM) // LANES) * LANES
     circle = sector * peers
-    forward, inverse, wavenumber = tables(circle, sector, width)
+    forward, inverse = tables(circle, sector, width)
     plane = rows * levels
-    limits = lax.dynamic_slice_in_dim(cutoff, lax.axis_index("lat") * rows, rows, 0)
-    limit = limits.astype(jnp.float32)[:, None]
-    number = jnp.asarray(wavenumber, jnp.float32)[None, :]
-    ratio = limit / jnp.maximum(number, 1.0)
-    damping = jnp.where(number > limit, ratio * ratio, 1.0)
-    couple = jnp.broadcast_to(
-        jnp.transpose(coupling, (1, 2, 0)).reshape(fields * fields, levels, 1), (fields * fields, levels, LANES)
-    )
     flat = [r.reshape(plane, sector) for r in (lat_ahead, lat_behind, lon_ahead, lon_behind)]
     vmem = pl.BlockSpec(memory_space=pltpu.VMEM)
-    anywhere = pl.BlockSpec(memory_space=pl.ANY)
+    hbm = pl.BlockSpec(memory_space=pltpu.HBM)
+    smem = pl.BlockSpec(memory_space=pltpu.SMEM)
     rim_slots = 1 if peers == 2 else 2
     packs = -(-(4 + fields) // 4)
     tall = rows + 2 * DEPTH
@@ -377,9 +408,11 @@
     out = pl.pallas_call(
         body,
         out_shape=jax.ShapeDtypeStruct((fields, plane, sector), jnp.float32),
-        in_specs=[vmem] * 7 + [anywhere] * 2,
+        in_specs=[hbm] * 5 + [smem] * 2 + [hbm] * 2,
         out_specs=vmem,
         scratch_shapes=[
+            pltpu.VMEM((fields, plane, sector), jnp.float32),
+            pltpu.VMEM((4, plane, sector), jnp.float32),
             pltpu.VMEM(forward.shape, jnp.bfloat16),
             pltpu.VMEM(inverse.shape, jnp.bfloat16),
             pltpu.VMEM((peers - 1, fields, plane, sector), jnp.float32),
@@ -392,14 +425,15 @@
             pltpu.VMEM((5, tall, levels, width), jnp.float32),
             pltpu.VMEM((fields * fields, levels, LANES), jnp.float32),
             pltpu.VMEM((SUBSTEPS + 1, fields, tall, levels, width), jnp.float32),
-            dma((2,)), dma((2, peers - 1)), dma((2, peers - 1)),
-            dma((rim_slots,)), dma((rim_slots,)),
+            pltpu.VMEM((rows, circle), jnp.float32),
+            dma((5,)), dma((2,)), dma((2, peers - 1)), dma((2, peers - 1)),
+            dma((2, rim_slots)), dma((2, rim_slots)),
             dma((2,)), dma((2,)), dma((rounds, 2)), dma((rounds, 2)),
         ],
         compiler_params=pltpu.CompilerParams(
             collective_id=0, has_side_effects=True, vmem_limit_bytes=48 * 1024 * 1024
         ),
-    )(adjoint_in.reshape(fields, plane, sector), *flat, couple, damping, jnp.asarray(forward), jnp.asarray(inverse))
+    )(adjoint_in.reshape(fields, plane, sector), *flat, coupling.reshape(-1), cutoff, jnp.asarray(forward), jnp.asarray(inverse))
     return out.reshape(fields, levels, rows, sector)
 
 

time: 64.1 us -> 58.4 us (0.911)
  Pallas kernels: 53.8 us -> 49 us
  other arithmetic: 1.52 us -> 0 us
    pallas_call x1, Pallas kernels: 53.8 us -> 49 us  [shards(): pl.pallas_call(body, out_shape=jax.ShapeDtypeStruct((fields, plane, secto...]
    unnamed x13 -> x16, local copies, waits for them, and re-layouts: 7.53 us -> 8.92 us
    transpose x1 -> x0, local copies, waits for them, and re-layouts: 0.83 us -> none  [shards(): jnp.transpose(coupling, (1, 2, 0)).reshape(fields * fields, levels, 1)]
    select_n x1 -> x0, other arithmetic: 0.79 us -> none  [shards(): damping = jnp.where(number > limit, ratio * ratio, 1.0)]
    convert_element_type x1 -> x0, other arithmetic: 0.73 us -> none  [shards(): limit = limits.astype(jnp.float32)[:, None]]
where the time goes in v1:
time: 58.4 us; the launch traced here: 58.1 us
  Pallas kernels  49 us (84%)
  local copies, waits for them, and re-layouts  9.03 us (15%)
    pallas_call x1, Pallas kernels, shards(): pl.pallas_call(body, out_shape=jax.ShapeDtypeStruct((fields, plane, secto...  49 us
    unnamed x16, local copies, waits for them, and re-layouts  8.92 us

profile of v1, /device:TPU:0, one launch (start us, length us, event | category | flops | bytes accessed | tf_op | source)
XLA Modules:
  0.0 58.1 jit_solution(12888379918856825328)
XLA Ops:
  0.0 0.7 %copy.10 = f32[8,5,5]{2,1,0:T(8,128)S(1)} copy(f32[8,5,5]{2,0,1:T(8,128)} %param.14) | data formatting | bytes 1600 | tf_op args[5]
  0.7 0.1 reshape.26.rest_0_
  0.8 0.0 copy-start
  0.9 1.8 %copy-done = bf16[2,1152,640]{2,1,0:T(8,128)(2,1)S(1)} copy-done((bf16[2,1152,640]{2,1,0:T(8,128)(2,1)S(1)}, bf16[2,1152,640]{2,1,0:T(8,128)(2,1)}, u32[]{:S(2)}) %copy-start) | copy-done | bytes 2949144
  2.7 0.0 copy-start.1
  2.7 1.1 %copy-done.1 = f32[5,8,8,576]{3,2,1,0:T(8,128)S(1)} copy-done((f32[5,8,8,576]{3,2,1,0:T(8,128)S(1)}, f32[5,8,8,576]{3,2,1,0:T(8,128)}, u32[]{:S(2)}) %copy-start.1) | copy-done | bytes 737304
  3.8 0.0 copy-start.2
  3.8 0.9 %copy-done.2 = f32[8,8,576]{2,1,0:T(8,128)S(1)} copy-done((f32[8,8,576]{2,1,0:T(8,128)S(1)}, f32[8,8,576]{2,1,0:T(8,128)}, u32[]{:S(2)}) %copy-start.2) | copy-done | bytes 147480
  4.7 0.0 copy-start.3
  4.7 0.9 %copy-done.3 = f32[8,8,576]{2,1,0:T(8,128)S(1)} copy-done((f32[8,8,576]{2,1,0:T(8,128)S(1)}, f32[8,8,576]{2,1,0:T(8,128)}, u32[]{:S(2)}) %copy-start.3) | copy-done | bytes 147480
  5.7 0.0 copy-start.4
  5.7 0.9 %copy-done.4 = f32[8,8,576]{2,1,0:T(8,128)S(1)} copy-done((f32[8,8,576]{2,1,0:T(8,128)S(1)}, f32[8,8,576]{2,1,0:T(8,128)}, u32[]{:S(2)}) %copy-start.4) | copy-done | bytes 147480
  6.6 0.0 copy-start.5
  6.6 0.9 %copy-done.5 = f32[8,8,576]{2,1,0:T(8,128)S(1)} copy-done((f32[8,8,576]{2,1,0:T(8,128)S(1)}, f32[8,8,576]{2,1,0:T(8,128)}, u32[]{:S(2)}) %copy-start.5) | copy-done | bytes 147480
  7.5 0.0 copy-start.6
  7.5 0.7 %copy-done.6 = s32[32]{0:T(128)S(1)} copy-done((s32[32]{0:T(128)S(1)}, s32[32]{0:T(128)}, u32[]{:S(2)}) %copy-start.6) | copy-done | bytes 152
  8.2 49.0 %shard_map.91 = f32[5,64,576]{2,1,0:T(8,128)S(1)} custom-call(f32[5,64,576]{2,1,0:T(8,128)S(1)} %bitcast.7, f32[64,576]{1,0:T(8,128)S(1)} %bitcast.8, f32[64,576]{1,0:T(8,128)S(1)} %bitcast.9, f32[64,576]{1,0:T(8,128)S(1)} %bitcast.10, f32[64,576]{1,0:T(8,128)S(1)} %bitcast.11, f32[200]{0:T(256)S(1)} %reshape.26.rest_0_, s32[32]{0:T(128)S(1)} %copy-done.6, ...), custom_call_target="tpu_custom_call" | custom-call | tf_op jit(solution)/shard_map/pallas_call | solution.py:408
  57.2 0.9 %copy.12 = f32[5,8,8,576]{3,2,1,0:T(8,128)} copy(f32[5,8,8,576]{3,2,1,0:T(8,128)S(1)} %bitcast.6) | data formatting | bytes 1474560
Async XLA Ops:
  0.8 1.8 %copy-start = (bf16[2,1152,640]{2,1,0:T(8,128)(2,1)S(1)}, bf16[2,1152,640]{2,1,0:T(8,128)(2,1)}, u32[]{:S(2)}) copy-start(bf16[2,1152,640]{2,1,0:T(8,128)(2,1)} %constant.5.clone.rest_3_) | copy-start | bytes 8847364
  2.7 1.1 %copy-start.1 = (f32[5,8,8,576]{3,2,1,0:T(8,128)S(1)}, f32[5,8,8,576]{3,2,1,0:T(8,128)}, u32[]{:S(2)}) copy-start(f32[5,8,8,576]{3,2,1,0:T(8,128)} %param.9) | copy-start | bytes 2211844
  3.8 0.9 %copy-start.2 = (f32[8,8,576]{2,1,0:T(8,128)S(1)}, f32[8,8,576]{2,1,0:T(8,128)}, u32[]{:S(2)}) copy-start(f32[8,8,576]{2,1,0:T(8,128)} %param.10) | copy-start | bytes 442372
  4.7 0.9 %copy-start.3 = (f32[8,8,576]{2,1,0:T(8,128)S(1)}, f32[8,8,576]{2,1,0:T(8,128)}, u32[]{:S(2)}) copy-start(f32[8,8,576]{2,1,0:T(8,128)} %param.11) | copy-start | bytes 442372
  5.7 0.9 %copy-start.4 = (f32[8,8,576]{2,1,0:T(8,128)S(1)}, f32[8,8,576]{2,1,0:T(8,128)}, u32[]{:S(2)}) copy-start(f32[8,8,576]{2,1,0:T(8,128)} %param.12) | copy-start | bytes 442372
  6.6 0.9 %copy-start.5 = (f32[8,8,576]{2,1,0:T(8,128)S(1)}, f32[8,8,576]{2,1,0:T(8,128)}, u32[]{:S(2)}) copy-start(f32[8,8,576]{2,1,0:T(8,128)} %param.13) | copy-start | bytes 442372
  7.5 0.7 %copy-start.6 = (s32[32]{0:T(128)S(1)}, s32[32]{0:T(128)}, u32[]{:S(2)}) copy-start(s32[32]{0:T(128)} %rest_1_.1) | copy-start | bytes 388

commit v2 on v1

--- a/solution.py
+++ b/solution.py
@@ -12,6 +12,7 @@
 DEPTH = 3
 RIM = 16
 LANES = 128
+VMEM_BYTES = 67_000_000
 MESH = pl.DeviceIdType.MESH
 
 
@@ -165,13 +166,9 @@
         for copy in field_rims:
             copy.start()
 
-    level_of = lax.broadcasted_iota(jnp.int32, (levels, LANES), 0)
-
     def entry(g, f):
-        value = jnp.full((levels, LANES), 1.0 if g == f else 0.0, jnp.float32)
-        for level in range(levels):
-            value = jnp.where(level_of == level, value + couple_ref[level * fields * fields + g * fields + f], value)
-        return value
+        value = jnp.broadcast_to(couple_ref[g, :, f:f + 1], (levels, LANES))
+        return value + 1.0 if g == f else value
 
     once = [[entry(g, f) for f in range(fields)] for g in range(fields)]
 
@@ -408,7 +405,7 @@
     out = pl.pallas_call(
         body,
         out_shape=jax.ShapeDtypeStruct((fields, plane, sector), jnp.float32),
-        in_specs=[hbm] * 5 + [smem] * 2 + [hbm] * 2,
+        in_specs=[hbm] * 5 + [vmem, smem] + [hbm] * 2,
         out_specs=vmem,
         scratch_shapes=[
             pltpu.VMEM((fields, plane, sector), jnp.float32),
@@ -431,9 +428,9 @@
             dma((2,)), dma((2,)), dma((rounds, 2)), dma((rounds, 2)),
         ],
         compiler_params=pltpu.CompilerParams(
-            collective_id=0, has_side_effects=True, vmem_limit_bytes=48 * 1024 * 1024
+            collective_id=0, has_side_effects=True, vmem_limit_bytes=VMEM_BYTES
         ),
-    )(adjoint_in.reshape(fields, plane, sector), *flat, coupling.reshape(-1), cutoff, jnp.asarray(forward), jnp.asarray(inverse))
+    )(adjoint_in.reshape(fields, plane, sector), *flat, jnp.transpose(coupling, (1, 0, 2)), cutoff, jnp.asarray(forward), jnp.asarray(inverse))
     return out.reshape(fields, levels, rows, sector)
 
 

time: 58.4 us -> 52.7 us (0.902)
  local copies, waits for them, and re-layouts: 9.03 us -> 2.1 us
  Pallas kernels: 49 us -> 50.3 us
    unnamed x16 -> x1, local copies, waits for them, and re-layouts: 8.92 us -> 2.1 us
    pallas_call x1, Pallas kernels: 49 us -> 50.3 us  [shards(): pl.pallas_call(body, out_shape=jax.ShapeDtypeStruct((fields, plane, secto...]
where the time goes in v2:
time: 52.7 us; the launch traced here: 52.5 us
  Pallas kernels  50.3 us (95%)
  local copies, waits for them, and re-layouts  2.1 us (4%)
    pallas_call x1, Pallas kernels, shards(): pl.pallas_call(body, out_shape=jax.ShapeDtypeStruct((fields, plane, secto...  50.3 us
    unnamed x1, local copies, waits for them, and re-layouts  2.1 us

profile of v2, /device:TPU:0, one launch (start us, length us, event | category | flops | bytes accessed | tf_op | source)
XLA Modules:
  0.0 52.5 jit_solution(15296233190970008994)
XLA Ops:
  0.0 50.3 %shard_map.91 = f32[5,64,576]{2,1,0:T(8,128)} custom-call(f32[5,64,576]{2,1,0:T(8,128)} %bitcast.8, f32[64,576]{1,0:T(8,128)} %bitcast.9, f32[64,576]{1,0:T(8,128)} %bitcast.10, f32[64,576]{1,0:T(8,128)} %bitcast.11, f32[64,576]{1,0:T(8,128)} %bitcast.12, f32[5,8,5]{2,1,0:T(8,128)} %bitcast.13, s32[32]{0:T(128)} %rest_1_.1, ...), custom_call_target="tpu_custom_call" | custom-call | tf_op jit(solution)/shard_map/pallas_call | solution.py:405
  50.4 2.1 %copy.11 = f32[5,8,8,576]{3,2,1,0:T(8,128)} copy(f32[5,8,8,576]{3,2,1,0:T(8,128)} %bitcast.7) | data formatting | bytes 1474560

commit v3 on v2

--- a/solution.py
+++ b/solution.py
@@ -9,7 +9,9 @@
 from jax.sharding import PartitionSpec as P
 
 SUBSTEPS = 6
-DEPTH = 3
+ROUNDS = (3, 3)
+DEPTH = ROUNDS[0]
+STARTS = tuple(sum(ROUNDS[:r]) for r in range(len(ROUNDS)))
 RIM = 16
 LANES = 128
 VMEM_BYTES = 67_000_000
@@ -52,16 +54,24 @@
 def kernel(
     peers, bands, fields, rows, levels, sector, width,
     x_hbm, rates_hbm, couple_ref, cutoff_ref, forward_hbm, inverse_hbm, out_ref,
-    x_ref, rate_ref, forward, inverse, swapped, spectra, filtered, rate_rows, packed, rim, rates, coefs, power, state, damp_ref,
-    load_sem, table_sem, swap_send, swap_recv, rim_send, rim_recv, rate_send, rate_recv, edge_send, edge_recv,
+    raw, raw_rim, raw_swap, x_ref, rate_ref, forward, inverse, swapped, spectra, filtered, rate_rows, packed, rim, rates, coefs, power, state, damp_ref,
+    raw_send, raw_recv, pass_send, pass_recv, load_sem, table_sem, swap_send, swap_recv, rim_send, rim_recv, rate_send, rate_recv, edge_send, edge_recv,
 ):
     chunks = 2
     lat = lax.axis_index("lat")
     lon = lax.axis_index("lon")
     quarter = bands // 4
-    polar = (lat < quarter) | (lat >= 3 * quarter)
+    depth = DEPTH
+
+    def in_polar(band):
+        return (band < quarter) | (band >= 3 * quarter)
+
+    polar = in_polar(lat)
     has_prev = lat > 0
     has_next = lat < bands - 1
+    prev_polar = has_prev & in_polar(lat - 1)
+    next_polar = has_next & in_polar(lat + 1)
+    filters = polar | prev_polar | next_polar
     plane = rows * levels
     part = plane // chunks
     tail = sector % LANES
@@ -93,7 +103,7 @@
         pltpu.make_async_copy(inverse_hbm, inverse, table_sem.at[1]),
     ]
 
-    @pl.when(polar)
+    @pl.when(filters)
     def _():
         for copy in table_copies:
             copy.start()
@@ -121,6 +131,45 @@
 
     for copy in loads:
         copy.wait()
+
+    def row_of(ref, j):
+        return jnp.concatenate(
+            [ref[t, pl.ds(j, levels, rows), :] for t in range(width // LANES)], axis=1
+        )
+
+    def raw_copy(side, row):
+        source = rows - depth + row if side == 0 else row
+        return pltpu.make_async_remote_copy(
+            src_ref=raw.at[:, source], dst_ref=raw_rim.at[side, :, row],
+            send_sem=raw_send.at[side, row], recv_sem=raw_recv.at[side, row],
+            device_id={"lat": lat + 1 if side == 0 else lat - 1}, device_id_type=MESH,
+        )
+
+    def pass_copy(side, row, d):
+        return pltpu.make_async_remote_copy(
+            src_ref=raw_rim.at[side, :, row], dst_ref=raw_swap.at[side, d - 1, :, row],
+            send_sem=pass_send.at[side, row, d - 1], recv_sem=pass_recv.at[side, row, d - 1],
+            device_id=lon_id(-d), device_id_type=MESH,
+        )
+
+    @pl.when(polar)
+    def _():
+        for f in range(fields):
+            for t in range(body // LANES):
+                filtered[f, t] = x_ref[f, :, t * LANES:(t + 1) * LANES]
+            filtered[f, body // LANES, :, 0:tail] = x_ref[f, :, body:sector]
+            for j in sorted({*range(depth), *range(rows - depth, rows)}):
+                raw[f, j] = row_of(filtered.at[f], j)[:, 0:sector]
+
+        @pl.when(has_next)
+        def _():
+            for row in range(depth):
+                raw_copy(0, row).start()
+
+        @pl.when(has_prev)
+        def _():
+            for row in range(depth):
+                raw_copy(1, row).start()
 
     sources = [r for r in rate_refs] + [x_ref.at[f] for f in range(fields)]
     lane = lax.broadcasted_iota(jnp.int32, (plane, LANES), 1)
@@ -185,18 +234,16 @@
         for f in range(fields):
             power[g * fields + f] = result[g][f]
 
-    depth = DEPTH
-
     @pl.when(jnp.logical_not(has_prev))
     def _():
         rates[:, 0:depth] = jnp.zeros((4, depth, levels, width), jnp.float32)
-        for s in range(0, SUBSTEPS, depth):
+        for s in STARTS:
             state[s, :, 0:depth] = jnp.zeros((fields, depth, levels, width), jnp.float32)
 
     @pl.when(jnp.logical_not(has_next))
     def _():
         rates[:, depth + rows:] = jnp.zeros((4, depth, levels, width), jnp.float32)
-        for s in range(0, SUBSTEPS, depth):
+        for s in STARTS:
             state[s, :, depth + rows:] = jnp.zeros((fields, depth, levels, width), jnp.float32)
 
     for copy in rate_rims:
@@ -216,105 +263,106 @@
             target[t] = source[:, t * LANES:(t + 1) * LANES]
         target[body // LANES] = last
 
-    def row_of(ref, j):
-        return jnp.concatenate(
-            [ref[t, pl.ds(j, levels, rows), :] for t in range(width // LANES)], axis=1
-        )
-
     for r in range(4):
         with_rim(r, rate_rows.at[r])
     for r in range(4):
         for j in range(rows):
             rates[r, depth + j] = row_of(rate_rows.at[r], j)
 
-    def to_neighbours(ref, send, recv):
+    def to_neighbours(ref, reach, send, recv, prev_gives=True, self_gives=True, next_gives=True):
         to_prev = pltpu.make_async_remote_copy(
-            src_ref=ref.at[:, pl.ds(depth, depth)], dst_ref=ref.at[:, pl.ds(depth + rows, depth)],
+            src_ref=ref.at[:, pl.ds(depth, reach)], dst_ref=ref.at[:, pl.ds(depth + rows, reach)],
             send_sem=send.at[0], recv_sem=recv.at[0],
             device_id={"lat": lat - 1}, device_id_type=MESH,
         )
         to_next = pltpu.make_async_remote_copy(
-            src_ref=ref.at[:, pl.ds(rows, depth)], dst_ref=ref.at[:, pl.ds(0, depth)],
+            src_ref=ref.at[:, pl.ds(depth + rows - reach, reach)], dst_ref=ref.at[:, pl.ds(depth - reach, reach)],
             send_sem=send.at[1], recv_sem=recv.at[1],
             device_id={"lat": lat + 1}, device_id_type=MESH,
         )
 
         def start():
-            pl.when(has_prev)(to_prev.start)
-            pl.when(has_next)(to_next.start)
+            pl.when(has_prev & self_gives)(to_prev.start)
+            pl.when(has_next & self_gives)(to_next.start)
 
         def arrive():
-            pl.when(has_next)(to_prev.wait_recv)
-            pl.when(has_prev)(to_next.wait_recv)
+            pl.when(has_next & next_gives)(to_prev.wait_recv)
+            pl.when(has_prev & prev_gives)(to_next.wait_recv)
 
         def sent():
-            pl.when(has_prev)(to_prev.wait_send)
-            pl.when(has_next)(to_next.wait_send)
+            pl.when(has_prev & self_gives)(to_prev.wait_send)
+            pl.when(has_next & self_gives)(to_next.wait_send)
 
         return start, arrive, sent
 
-    rate_start, rate_arrive, rate_sent = to_neighbours(rates, rate_send, rate_recv)
+    rate_start, rate_arrive, rate_sent = to_neighbours(rates, depth, rate_send, rate_recv)
     rate_start()
 
-    @pl.when(jnp.logical_not(polar))
-    def _():
-        for copy in field_rims:
-            copy.wait()
-        for f in range(fields):
-            with_rim(4 + f, filtered.at[f])
-
-    modes = peers * sector
-
-    @pl.when(polar)
-    def _():
-        column = lax.broadcasted_iota(jnp.int32, (rows, modes), 1)
-        row_index = lax.broadcasted_iota(jnp.int32, (rows, modes), 0)
-        number = jnp.where(column <= modes // 2, column, column - modes // 2).astype(jnp.float32)
-        limit = jnp.zeros((rows, modes), jnp.float32)
-        for j in range(rows):
-            limit = jnp.where(row_index == j, cutoff_ref[lat * rows + j].astype(jnp.float32), limit)
-        ratio = limit / jnp.maximum(number, 1.0)
-        damp_ref[...] = jnp.where(number > limit, ratio * ratio, 1.0)
-        for copy in table_copies:
-            copy.wait()
-        for c in range(chunks):
-            own = x_ref[:, c * part:(c + 1) * part].reshape(fields * part, sector)
-            spectra[c] = product(own, forward[0, 0:sector], forward[1, 0:sector])
-        for c in range(chunks):
-            for copy in swaps[c]:
-                copy.wait_recv()
-            total = spectra[c]
-            for d in range(1, peers):
-                values = swapped[d - 1, :, c * part:(c + 1) * part].reshape(fields * part, sector)
-                start, end = d * sector, (d + 1) * sector
-                total = total + product(values, forward[0, start:end], forward[1, start:end])
-            damped = total.reshape(fields * part // rows, rows, modes) * damp_ref[...][None]
-            result = product(damped.reshape(fields * part, modes), inverse[0], inverse[1])
-            for t in range(width // LANES):
-                block = result[:, t * LANES:(t + 1) * LANES].reshape(fields, part, LANES)
-                filtered[:, t, c * part:(c + 1) * part] = block
-
-    edges = [
-        to_neighbours(state.at[s], edge_send.at[s // depth], edge_recv.at[s // depth])
-        for s in range(0, SUBSTEPS, depth)
-    ]
-
-    def couple(j):
-        values = [row_of(filtered.at[g], j) for g in range(fields)]
+    edges = []
+    for r, reach in enumerate(ROUNDS):
+        gives = (True, True, True)
+        if r == 0:
+            gives = tuple(jnp.logical_not(p) for p in (prev_polar, polar, next_polar))
+        edges.append(to_neighbours(state.at[STARTS[r]], reach, edge_send.at[r], edge_recv.at[r], *gives))
+
+    def mix(values, target):
         for f in range(fields):
             total = None
             for g in range(fields):
                 term = jnp.tile(power[g * fields + f], (1, width // LANES)) * values[g]
                 total = term if total is None else total + term
-            state[0, f, depth + j] = total
-
-    outer = list(range(depth)) + list(range(rows - depth, rows))
-    inner = list(range(depth, rows - depth))
-    for j in outer:
-        couple(j)
-    edges[0][0]()
-    for j in inner:
-        couple(j)
+            state[0, f, target] = total
+
+    def couple(j):
+        mix([row_of(filtered.at[g], j) for g in range(fields)], depth + j)
+
+    outer = sorted({*range(depth), *range(rows - depth, rows)})
+    inner = [j for j in range(rows) if j not in outer]
+
+    @pl.when(jnp.logical_not(polar))
+    def _():
+        for copy in field_rims:
+            copy.wait()
+        for f in range(fields):
+            with_rim(4 + f, filtered.at[f])
+        for j in outer:
+            couple(j)
+        edges[0][0]()
+        for j in inner:
+            couple(j)
+
+    sides = ((0, prev_polar), (1, next_polar))
+    for side, present in sides:
+        @pl.when(present)
+        def _():
+            for row in range(depth):
+                raw_copy(side, row).wait_recv()
+                for d in range(1, peers):
+                    pass_copy(side, row, d).start()
+
+    modes = peers * sector
+
+    def damping(shape, limit):
+        column = lax.broadcasted_iota(jnp.int32, shape, 1)
+        number = jnp.where(column <= modes // 2, column, column - modes // 2).astype(jnp.float32)
+        ratio = limit / jnp.maximum(number, 1.0)
+        return jnp.where(number > limit, ratio * ratio, 1.0)
+
+    @pl.when(filters)
+    def _():
+        for copy in table_copies:
+            copy.wait()
+
+    @pl.when(polar)
+    def _():
+        row_index = lax.broadcasted_iota(jnp.int32, (rows, modes), 0)
+        limit = jnp.zeros((rows, modes), jnp.float32)
+        for j in range(rows):
+            limit = jnp.where(row_index == j, cutoff_ref[lat * rows + j].astype(jnp.float32), limit)
+        damp_ref[...] = damping((rows, modes), limit)
+        for c in range(chunks):
+            own = x_ref[:, c * part:(c + 1) * part].reshape(fields * part, sector)
+            spectra[c] = product(own, forward[0, 0:sector], forward[1, 0:sector])
 
     rate_arrive()
     below_last = jnp.where(has_next, 1.0, 0.0)
@@ -331,6 +379,45 @@
         coefs[3, j] = north
         coefs[4, j] = south
 
+    @pl.when(polar)
+    def _():
+        for c in range(chunks):
+            for copy in swaps[c]:
+                copy.wait_recv()
+            total = spectra[c]
+            for d in range(1, peers):
+                values = swapped[d - 1, :, c * part:(c + 1) * part].reshape(fields * part, sector)
+                start, end = d * sector, (d + 1) * sector
+                total = total + product(values, forward[0, start:end], forward[1, start:end])
+            damped = total.reshape(fields * part // rows, rows, modes) * damp_ref[...][None]
+            result = product(damped.reshape(fields * part, modes), inverse[0], inverse[1])
+            for t in range(width // LANES):
+                block = result[:, t * LANES:(t + 1) * LANES].reshape(fields, part, LANES)
+                filtered[:, t, c * part:(c + 1) * part] = block
+        for j in range(rows):
+            couple(j)
+
+    for side, present in sides:
+        @pl.when(present)
+        def _():
+            count = fields * depth * levels
+            total = product(raw_rim[side].reshape(count, sector), forward[0, 0:sector], forward[1, 0:sector])
+            for d in range(1, peers):
+                for row in range(depth):
+                    pass_copy(side, row, d).wait_recv()
+                start, end = d * sector, (d + 1) * sector
+                total = total + product(
+                    raw_swap[side, d - 1].reshape(count, sector), forward[0, start:end], forward[1, start:end]
+                )
+            begin = lat * rows - depth if side == 0 else (lat + 1) * rows
+            limits = [cutoff_ref[begin + row].astype(jnp.float32) for row in range(depth)]
+            table = jnp.stack([damping((levels, modes), limit) for limit in limits])
+            damped = total.reshape(fields, depth, levels, modes) * table[None]
+            result = product(damped.reshape(count, modes), inverse[0], inverse[1])
+            result = result.reshape(fields, depth, levels, width)
+            for row in range(depth):
+                mix([result[g, row] for g in range(fields)], row if side == 0 else depth + rows + row)
+
     def advance(s, j):
         rate = [coefs[k, j] for k in range(5)]
         for f in range(fields):
@@ -350,18 +437,19 @@
             def _(j):
                 advance(s, j)
 
-    for s in range(SUBSTEPS):
-        reach = depth - 1 - s % depth
-        begin, end = depth - reach, depth + rows + reach
-        if s % depth == 0:
-            edges[s // depth][1]()
-        if (s + 1) % depth == 0 and s + 1 < SUBSTEPS:
-            advance_rows(s, depth, 2 * depth)
-            advance_rows(s, rows, rows + depth)
-            edges[(s + 1) // depth][0]()
-            advance_rows(s, 2 * depth, rows)
-        else:
-            advance_rows(s, begin, end)
+    for r, first in enumerate(STARTS):
+        edges[r][1]()
+        for k in range(ROUNDS[r]):
+            s = first + k
+            reach = ROUNDS[r] - 1 - k
+            if reach == 0 and s + 1 < SUBSTEPS:
+                ahead = ROUNDS[r + 1]
+                advance_rows(s, depth, depth + ahead)
+                advance_rows(s, depth + rows - ahead, depth + rows)
+                edges[r + 1][0]()
+                advance_rows(s, depth + ahead, depth + rows - ahead)
+            else:
+                advance_rows(s, depth - reach, depth + rows + reach)
 
     for f in range(fields):
         for j in range(rows):
@@ -381,6 +469,23 @@
         for c in range(chunks):
             for copy in swaps[c]:
                 copy.wait_send()
+
+        @pl.when(has_next)
+        def _():
+            for row in range(depth):
+                raw_copy(0, row).wait_send()
+
+        @pl.when(has_prev)
+        def _():
+            for row in range(depth):
+                raw_copy(1, row).wait_send()
+
+    for side, present in sides:
+        @pl.when(present)
+        def _():
+            for row in range(depth):
+                for d in range(1, peers):
+                    pass_copy(side, row, d).wait_send()
 
 
 def shards(peers, bands, adjoint_in, lat_ahead, lat_behind, lon_ahead, lon_behind, coupling, cutoff):
@@ -396,7 +501,7 @@
     rim_slots = 1 if peers == 2 else 2
     packs = -(-(4 + fields) // 4)
     tall = rows + 2 * DEPTH
-    rounds = SUBSTEPS // DEPTH
+    rounds = len(ROUNDS)
 
     def body(x, a, b, c, d, *rest):
         kernel(peers, bands, fields, rows, levels, sector, width, x, [a, b, c, d], *rest)
@@ -408,6 +513,9 @@
         in_specs=[hbm] * 5 + [vmem, smem] + [hbm] * 2,
         out_specs=vmem,
         scratch_shapes=[
+            pltpu.VMEM((fields, rows, levels, sector), jnp.float32),
+            pltpu.VMEM((2, fields, DEPTH, levels, sector), jnp.float32),
+            pltpu.VMEM((2, peers - 1, fields, DEPTH, levels, sector), jnp.float32),
             pltpu.VMEM((fields, plane, sector), jnp.float32),
             pltpu.VMEM((4, plane, sector), jnp.float32),
             pltpu.VMEM(forward.shape, jnp.bfloat16),
@@ -423,6 +531,7 @@
             pltpu.VMEM((fields * fields, levels, LANES), jnp.float32),
             pltpu.VMEM((SUBSTEPS + 1, fields, tall, levels, width), jnp.float32),
             pltpu.VMEM((rows, circle), jnp.float32),
+            dma((2, DEPTH)), dma((2, DEPTH)), dma((2, DEPTH, peers - 1)), dma((2, DEPTH, peers - 1)),
             dma((5,)), dma((2,)), dma((2, peers - 1)), dma((2, peers - 1)),
             dma((2, rim_slots)), dma((2, rim_slots)),
             dma((2,)), dma((2,)), dma((rounds, 2)), dma((rounds, 2)),

time: 52.7 us -> 43.5 us (0.83)
  the two profiles are of different devices: /device:TPU:0 before, /device:TPU:16 now
where the time goes in v3:
time: 43.5 us; the launch traced here: 43.3 us
  Pallas kernels  41.2 us (95%)
  local copies, waits for them, and re-layouts  2.1 us (5%)
    pallas_call x1, Pallas kernels, shards(): pl.pallas_call(body, out_shape=jax.ShapeDtypeStruct((fields, plane, secto...  41.2 us
    unnamed x1, local copies, waits for them, and re-layouts  2.1 us

profile of v3, /device:TPU:16, one launch (start us, length us, event | category | flops | bytes accessed | tf_op | source)
XLA Modules:
  0.0 43.3 jit_solution(2638274935282958102)
XLA Ops:
  0.0 41.2 %shard_map.91 = f32[5,64,576]{2,1,0:T(8,128)} custom-call(f32[5,64,576]{2,1,0:T(8,128)} %bitcast.8, f32[64,576]{1,0:T(8,128)} %bitcast.9, f32[64,576]{1,0:T(8,128)} %bitcast.10, f32[64,576]{1,0:T(8,128)} %bitcast.11, f32[64,576]{1,0:T(8,128)} %bitcast.12, f32[5,8,5]{2,1,0:T(8,128)} %bitcast.13, s32[32]{0:T(128)} %rest_1_.1, ...), custom_call_target="tpu_custom_call" | custom-call | tf_op jit(solution)/shard_map/pallas_call | solution.py:510
  41.2 2.1 %copy.11 = f32[5,8,8,576]{3,2,1,0:T(8,128)} copy(f32[5,8,8,576]{3,2,1,0:T(8,128)} %bitcast.7) | data formatting | bytes 1474560

commit v4 on v3

--- a/solution.py
+++ b/solution.py
@@ -9,12 +9,12 @@
 from jax.sharding import PartitionSpec as P
 
 SUBSTEPS = 6
-ROUNDS = (3, 3)
+ROUNDS = (4, 2)
 DEPTH = ROUNDS[0]
 STARTS = tuple(sum(ROUNDS[:r]) for r in range(len(ROUNDS)))
 RIM = 16
 LANES = 128
-VMEM_BYTES = 67_000_000
+VMEM_BYTES = 66_200_000
 MESH = pl.DeviceIdType.MESH
 
 
@@ -295,8 +295,14 @@
 
         return start, arrive, sent
 
-    rate_start, rate_arrive, rate_sent = to_neighbours(rates, depth, rate_send, rate_recv)
+    rate_start, rate_arrive, rate_sent = to_neighbours(rates, depth - 1, rate_send, rate_recv)
+    behind = pltpu.make_async_remote_copy(
+        src_ref=rates.at[1, rows], dst_ref=rates.at[1, 0],
+        send_sem=rate_send.at[2], recv_sem=rate_recv.at[2],
+        device_id={"lat": lat + 1}, device_id_type=MESH,
+    )
     rate_start()
+    pl.when(has_next)(behind.start)
 
     edges = []
     for r, reach in enumerate(ROUNDS):
@@ -365,6 +371,7 @@
             spectra[c] = product(own, forward[0, 0:sector], forward[1, 0:sector])
 
     rate_arrive()
+    pl.when(has_prev)(behind.wait_recv)
     below_last = jnp.where(has_next, 1.0, 0.0)
     for j in range(1, rows + 2 * depth - 1):
         north = rates[0, j]
@@ -461,6 +468,7 @@
         out_ref[:, :, t * LANES:end] = filtered[:, t, :, 0:end - t * LANES]
 
     rate_sent()
+    pl.when(has_next)(behind.wait_send)
     for edge in edges:
         edge[2]()
 
@@ -534,7 +542,7 @@
             dma((2, DEPTH)), dma((2, DEPTH)), dma((2, DEPTH, peers - 1)), dma((2, DEPTH, peers - 1)),
             dma((5,)), dma((2,)), dma((2, peers - 1)), dma((2, peers - 1)),
             dma((2, rim_slots)), dma((2, rim_slots)),
-            dma((2,)), dma((2,)), dma((rounds, 2)), dma((rounds, 2)),
+            dma((3,)), dma((3,)), dma((rounds, 2)), dma((rounds, 2)),
         ],
         compiler_params=pltpu.CompilerParams(
             collective_id=0, has_side_effects=True, vmem_limit_bytes=VMEM_BYTES

time: 43.5 us -> 41.9 us (0.963)
  the two profiles are of different devices: /device:TPU:16 before, /device:TPU:0 now
where the time goes in v4:
time: 41.9 us; the launch traced here: 41.7 us
  Pallas kernels  39.6 us (95%)
  local copies, waits for them, and re-layouts  2.1 us (5%)
    pallas_call x1, Pallas kernels, shards(): pl.pallas_call(body, out_shape=jax.ShapeDtypeStruct((fields, plane, secto...  39.6 us
    unnamed x1, local copies, waits for them, and re-layouts  2.1 us

profile of v4, /device:TPU:0, one launch (start us, length us, event | category | flops | bytes accessed | tf_op | source)
XLA Modules:
  0.0 41.7 jit_solution(8852860430544771065)
XLA Ops:
  0.0 39.6 %shard_map.91 = f32[5,64,576]{2,1,0:T(8,128)} custom-call(f32[5,64,576]{2,1,0:T(8,128)} %bitcast.8, f32[64,576]{1,0:T(8,128)} %bitcast.9, f32[64,576]{1,0:T(8,128)} %bitcast.10, f32[64,576]{1,0:T(8,128)} %bitcast.11, f32[64,576]{1,0:T(8,128)} %bitcast.12, f32[5,8,5]{2,1,0:T(8,128)} %bitcast.13, s32[32]{0:T(128)} %rest_1_.1, ...), custom_call_target="tpu_custom_call" | custom-call | tf_op jit(solution)/shard_map/pallas_call | solution.py:518
  39.6 2.1 %copy.11 = f32[5,8,8,576]{3,2,1,0:T(8,128)} copy(f32[5,8,8,576]{3,2,1,0:T(8,128)} %bitcast.7) | data formatting | bytes 1474560

commit v5 on v4

--- a/solution.py
+++ b/solution.py
@@ -440,9 +440,10 @@
 
     def advance_rows(s, start, end):
         if end > start:
-            @pl.loop(start, end)
+            @pl.loop(start, end, step=2)
             def _(j):
                 advance(s, j)
+                advance(s, j + 1)
 
     for r, first in enumerate(STARTS):
         edges[r][1]()
@@ -517,7 +518,7 @@
     dma = pltpu.SemaphoreType.DMA
     out = pl.pallas_call(
         body,
-        out_shape=jax.ShapeDtypeStruct((fields, plane, sector), jnp.float32),
+        out_shape=pltpu.VMEM((fields, plane, sector), jnp.float32),
         in_specs=[hbm] * 5 + [vmem, smem] + [hbm] * 2,
         out_specs=vmem,
         scratch_shapes=[

time: 41.9 us -> 37.7 us (0.90)
  Pallas kernels: 39.6 us -> 36.6 us
  local copies, waits for them, and re-layouts: 2.1 us -> 0.89 us
    pallas_call x1, Pallas kernels: 39.6 us -> 36.6 us  [shards(): pl.pallas_call(body, out_shape=pltpu.VMEM((fields, plane, sector), jnp.fl...]
    unnamed x1, local copies, waits for them, and re-layouts: 2.1 us -> 0.89 us
where the time goes in v5:
time: 37.7 us; the launch traced here: 37.5 us
  Pallas kernels  36.6 us (97%)
  local copies, waits for them, and re-layouts  0.89 us (2%)
    pallas_call x1, Pallas kernels, shards(): pl.pallas_call(body, out_shape=pltpu.VMEM((fields, plane, sector), jnp.fl...  36.6 us
    unnamed x1, local copies, waits for them, and re-layouts  0.89 us

profile of v5, /device:TPU:0, one launch (start us, length us, event | category | flops | bytes accessed | tf_op | source)
XLA Modules:
  0.0 37.5 jit_solution(2634731320570283892)
XLA Ops:
  0.0 36.6 %shard_map.91 = f32[5,64,576]{2,1,0:T(8,128)S(1)} custom-call(f32[5,64,576]{2,1,0:T(8,128)} %bitcast.8, f32[64,576]{1,0:T(8,128)} %bitcast.9, f32[64,576]{1,0:T(8,128)} %bitcast.10, f32[64,576]{1,0:T(8,128)} %bitcast.11, f32[64,576]{1,0:T(8,128)} %bitcast.12, f32[5,8,5]{2,1,0:T(8,128)} %bitcast.13, s32[32]{0:T(128)} %rest_1_.1, ...), custom_call_target="tpu_custom_call" | custom-call | tf_op jit(solution)/shard_map/pallas_call | solution.py:519
  36.6 0.9 %copy.11 = f32[5,8,8,576]{3,2,1,0:T(8,128)} copy(f32[5,8,8,576]{3,2,1,0:T(8,128)S(1)} %bitcast.7) | data formatting | bytes 1474560

commit v6 on v5

--- a/solution.py
+++ b/solution.py
@@ -9,7 +9,7 @@
 from jax.sharding import PartitionSpec as P
 
 SUBSTEPS = 6
-ROUNDS = (4, 2)
+ROUNDS = (5, 1)
 DEPTH = ROUNDS[0]
 STARTS = tuple(sum(ROUNDS[:r]) for r in range(len(ROUNDS)))
 RIM = 16
@@ -439,11 +439,15 @@
             state[s + 1, f, j] = value
 
     def advance_rows(s, start, end):
-        if end > start:
-            @pl.loop(start, end, step=2)
+        half = (end - start) // 2
+        if half < 2 or (end - start) % 2:
+            for j in range(start, end):
+                advance(s, j)
+        else:
+            @pl.loop(start, end, step=half)
             def _(j):
-                advance(s, j)
-                advance(s, j + 1)
+                for offset in range(half):
+                    advance(s, j + offset)
 
     for r, first in enumerate(STARTS):
         edges[r][1]()

time: 37.7 us -> 39 us (1.034)
  Pallas kernels: 36.6 us -> 37.8 us
    pallas_call x1, Pallas kernels: 36.6 us -> 37.8 us  [shards(): pl.pallas_call(body, out_shape=pltpu.VMEM((fields, plane, sector), jnp.fl...]
where the time goes in v6:
time: 39 us; the launch traced here: 38.7 us
  Pallas kernels  37.8 us (97%)
  local copies, waits for them, and re-layouts  0.89 us (2%)
    pallas_call x1, Pallas kernels, shards(): pl.pallas_call(body, out_shape=pltpu.VMEM((fields, plane, sector), jnp.fl...  37.8 us
    unnamed x1, local copies, waits for them, and re-layouts  0.89 us

profile of v6, /device:TPU:0, one launch (start us, length us, event | category | flops | bytes accessed | tf_op | source)
XLA Modules:
  0.0 38.7 jit_solution(16537209594624329282)
XLA Ops:
  0.0 37.8 %shard_map.91 = f32[5,64,576]{2,1,0:T(8,128)S(1)} custom-call(f32[5,64,576]{2,1,0:T(8,128)} %bitcast.8, f32[64,576]{1,0:T(8,128)} %bitcast.9, f32[64,576]{1,0:T(8,128)} %bitcast.10, f32[64,576]{1,0:T(8,128)} %bitcast.11, f32[64,576]{1,0:T(8,128)} %bitcast.12, f32[5,8,5]{2,1,0:T(8,128)} %bitcast.13, s32[32]{0:T(128)} %rest_1_.1, ...), custom_call_target="tpu_custom_call" | custom-call | tf_op jit(solution)/shard_map/pallas_call | solution.py:523
  37.8 0.9 %copy.11 = f32[5,8,8,576]{3,2,1,0:T(8,128)} copy(f32[5,8,8,576]{3,2,1,0:T(8,128)S(1)} %bitcast.7) | data formatting | bytes 1474560
